TPU v7x, 32 devices: a whole 2x2x4 slice. The times are simulated.
32 devices in a mesh: graph: 16 (over z, y, x), rep: 2 (over core).
Axes of the slice: x: 2, y: 2, z: 4, core: 2. Of those that a mesh axis runs over, the one named last changes fastest.
Arguments:
- grad_out: bfloat16 [8192, 256], P(('graph', 'rep')), may hold values from -6 to 6
- pre_act: bfloat16 [8192, 256], P(('graph', 'rep')), may hold values from -6 to 6
- aggregated: bfloat16 [8192, 256], P(('graph', 'rep')), may hold values from -0.3125 to 0.3125
- weight: bfloat16 [256, 256], replicated, may hold values from -0.375 to 0.375
- adj_tiles: bfloat16 [16, 2, 16, 2, 128, 128], P('graph', 'rep'), may hold values from 0 to 0.039794922
- tile_row: int32 [16, 2, 16, 2], P('graph', 'rep'), may hold values from 0 to 1
- tile_col: int32 [16, 2, 16, 2], P('graph', 'rep'), may hold values from 0 to 3
- tile_count: int32 [16, 2, 16], P('graph', 'rep'), may hold values from 0 to 2, as said below
- node_perm: int32 [16, 512], P('graph'), may hold values from 0 to 511, each once within a row
Outputs:
- input_grad: bfloat16 [8192, 256], P(('graph', 'rep'))
- weight_grad: float32 [256, 256], replicated
- relu_grad: bfloat16 [8192, 256], P(('graph', 'rep'))
Inputs may be any that keep to these rules, and one draw needn't show every extreme that they name: tile_count[g, r, g] is 2 for every partition g and replica r. `node_perm`: each row is a permutation.
All inputs are finite; a program needn't handle non-finite values.
Results may differ from a plain program's by a relative error of at most 0.0049.
Values may be sent and summed in bfloat16 or wider, within the bound.
A program may use at most 128 MiB of HBM per device.

v0:
```python
import jax
import jax.numpy as jnp
from jax import lax
from jax.sharding import PartitionSpec as P


def tile_products(running, sources, row_count, local_tiles, local_row, local_col, local_count):
    piece_parts = sources.shape[0] // row_count
    tile_size = local_tiles.shape[-1]
    feature_width = sources.shape[1]
    blocks = sources.reshape(piece_parts, row_count // tile_size, tile_size, feature_width)
    part_index = jnp.arange(piece_parts, dtype=jnp.int32)
    for slot_index in range(local_tiles.shape[1]):
        chosen = blocks[part_index, local_row[:, slot_index]]
        product = jnp.einsum(
            "kab,kac->kbc", local_tiles[:, slot_index], chosen, preferred_element_type=jnp.float32
        )
        alive = (local_count > slot_index).astype(jnp.float32)
        running = running.at[local_col[:, slot_index]].add(product * alive[:, None, None])
    return running


def body(
    grad_out, pre_act, aggregated, weight, adj_tiles, tile_row, tile_col, tile_count, node_perm
):
    row_count = grad_out.shape[0]
    feature_width = weight.shape[0]
    relu_grad = jnp.where(pre_act > 0, grad_out, jnp.zeros_like(grad_out))
    partial_weight = lax.dot_general(
        aggregated, relu_grad, (((0,), (0,)), ((), ())), preferred_element_type=jnp.float32
    )
    local_tiles = adj_tiles[0, 0]
    local_row = tile_row[0, 0]
    local_col = tile_col[0, 0]
    local_count = tile_count[0, 0]
    local_perm = node_perm[0]
    tile_size = local_tiles.shape[-1]
    col_blocks = lax.axis_size("rep") * (row_count // tile_size)
    empty = jnp.zeros((col_blocks, tile_size, feature_width), jnp.float32)
    back_agg = lax.dot_general(
        relu_grad, weight, (((1,), (1,)), ((), ())), preferred_element_type=jnp.float32
    ).astype(jnp.bfloat16)
    running = tile_products(
        empty,
        lax.all_gather(back_agg, "graph", axis=0, tiled=True),
        row_count,
        local_tiles,
        local_row,
        local_col,
        local_count,
    )
    partial_grad = running.reshape(col_blocks * tile_size, feature_width)
    input_grad = lax.psum_scatter(
        jnp.take(partial_grad, local_perm, axis=0), "rep", scatter_dimension=0, tiled=True
    ).astype(jnp.bfloat16)
    weight_grad = lax.psum(partial_weight, ("graph", "rep"))
    return (input_grad, weight_grad, relu_grad)


def solution(mesh):
    placed = (
        P(("graph", "rep"), None),
        P(("graph", "rep"), None),
        P(("graph", "rep"), None),
        P(),
        P("graph", "rep", None, None, None, None),
        P("graph", "rep", None, None),
        P("graph", "rep", None, None),
        P("graph", "rep", None),
        P("graph", None),
    )
    return jax.shard_map(
        body,
        mesh=mesh,
        in_specs=placed,
        out_specs=(P(("graph", "rep"), None), P(), P(("graph", "rep"), None)),
        check_vma=False,
    )
```

profile of v0, /device:TPU:0, one launch (start us, length us, event | category | flops | bytes accessed | tf_op | source)
XLA Modules:
  0.0 160.9 jit_solution(16786216906860122379)
XLA Ops:
  8.1 1.1 compare_select_fusion
  9.2 0.9 convolution_convert_fusion
  10.1 0.0 all-reduce.2.cloned.1.call-start
  10.1 1.8 %convolution_bitcast_fusion = f32[256,256]{0,1:T(8,128)} fusion(bf16[256,256]{1,0:T(8,128)(2,1)S(1)} %compare_select_fusion, bf16[256,256]{1,0:T(8,128)(2,1)} %param.11), kind=kOutput, calls=%fused_computation.7 | convolution fusion | flops 33554432 | bytes 524288 | tf_op jit(solution)/shard_map/dot_general | solution.py:29
  12.0 0.7 compare_select_fusion.1
  12.7 0.7 compare_and_fusion
  13.4 0.8 fusion.10
  14.2 0.8 fusion.6
  14.9 0.7 fusion.1
  15.6 0.1 copy.25
  15.7 60.0 %all-gather.2.cloned.1.call-done = bf16[4096,256]{1,0:T(8,128)(2,1)} async-done(((bf16[256,256]{1,0:T(8,128)(2,1)}), bf16[4096,256]{1,0:T(8,128)(2,1)}) %all-gather.2.cloned.1.call-update) | async-done | bytes 2097168 | tf_op jit(solution)/shard_map/all_gather | solution.py:45
  75.7 3.2 %gather_fusion.1 = bf16[16,128,256]{2,1,0:T(8,128)(2,1)} fusion(bf16[16,2,128,256]{3,2,1,0:T(8,128)(2,1)} %bitcast.44, s32[16]{0:T(128)S(1)} %get-tuple-element.9), kind=kCustom, calls=%fused_computation.1 | custom fusion | bytes 2097280 | tf_op jit(solution)/shard_map/gather | solution.py:14
  78.9 2.2 %gather_fusion = bf16[16,128,256]{2,1,0:T(8,128)(2,1)S(1)} fusion(bf16[16,2,128,256]{3,2,1,0:T(8,128)(2,1)} %bitcast.45, s32[16]{0:T(128)S(1)} %get-tuple-element.10), kind=kCustom, calls=%fused_computation | custom fusion | bytes 2097280 | tf_op jit(solution)/shard_map/gather | solution.py:14
  81.1 1.8 %multiply_bitcast_fusion.1 = f32[16,128,256]{1,2,0:T(8,128)} fusion(bf16[16,128,256]{2,1,0:T(8,128)(2,1)S(1)} %gather_fusion, f32[16]{0:T(128)S(1)} %get-tuple-element.14, bf16[16,2,128,128]{3,2,0,1:T(8,128)(2,1)S(1)} %bitcast.42), kind=kOutput, calls=%fused_computation.6 | convolution fusion | flops 134742016 | bytes 3670528 | tf_op jit(solution)/shard_map/kab,kac->kbc/dot_general | solution.py:15
  83.0 1.9 %copy.18 = f32[16,128,256]{2,1,0:T(8,128)S(1)} copy(f32[16,128,256]{1,2,0:T(8,128)} %multiply_bitcast_fusion.1) | data formatting | bytes 4194304 | tf_op jit(solution)/shard_map/mul | solution.py:19
  84.9 3.1 %multiply_bitcast_fusion = f32[16,128,256]{1,2,0:T(8,128)} fusion(bf16[16,128,256]{2,1,0:T(8,128)(2,1)} %gather_fusion.1, f32[16]{0:T(128)S(1)} %get-tuple-element.13, bf16[16,2,128,128]{3,2,0,1:T(8,128)(2,1)S(1)} %bitcast.43), kind=kOutput, calls=%fused_computation.5 | convolution fusion | flops 134742016 | bytes 3670528 | tf_op jit(solution)/shard_map/kab,kac->kbc/dot_general | solution.py:15
  88.0 2.9 %copy.20 = f32[16,128,256]{2,1,0:T(8,128)} copy(f32[16,128,256]{1,2,0:T(8,128)} %multiply_bitcast_fusion) | data formatting | bytes 4194304 | tf_op jit(solution)/shard_map/mul | solution.py:19
  90.9 2.2 %scatter_fusion = f32[4,128,256]{2,1,0:T(8,128)S(1)} fusion(f32[4,128,256]{2,1,0:T(8,128)S(1)} %broadcast_in_dim.10, s32[16]{0:T(128)S(1)} %get-tuple-element.12, f32[16,128,256]{2,1,0:T(8,128)S(1)} %copy.18), kind=kCustom, calls=%fused_computation.3 | custom fusion | flops 524288 | bytes 6291520 | tf_op jit(solution)/shard_map/scatter-add | solution.py:19
  93.1 3.5 %scatter_fusion.1 = f32[4,128,256]{2,1,0:T(8,128)S(1)} fusion(f32[4,128,256]{2,1,0:T(8,128)S(1)} %scatter_fusion, s32[16]{0:T(128)S(1)} %get-tuple-element.11, f32[16,128,256]{2,1,0:T(8,128)} %copy.20), kind=kCustom, calls=%fused_computation.4 | custom fusion | flops 524288 | bytes 6291520 | tf_op jit(solution)/shard_map/scatter-add | solution.py:19
  96.6 1.6 gather_fusion.2
  98.2 0.9 broadcast_select_fusion
  99.1 51.0 %all-reduce.2.cloned.1.call-done = f32[256,256]{0,1:T(8,128)} async-done(((f32[256,256]{0,1:T(8,128)}), f32[256,256]{0,1:T(8,128)}) %all-reduce.2.cloned.1.call-update) | async-done | bytes 262160 | tf_op jit(solution)/shard_map/psum | solution.py:56
  150.1 1.8 %copy.21 = f32[256,256]{1,0:T(8,128)} copy(f32[256,256]{0,1:T(8,128)} %all-reduce.2.cloned.1.call-done) | data formatting | bytes 524288
  151.9 1.6 %convert_element_type.31 = bf16[256,256]{1,0:T(8,128)(2,1)} convert(f32[256,256]{1,0:T(8,128)} %reduce-scatter.2.cloned.1.call-done) | non-fusion elementwise | flops 65536 | bytes 393216 | tf_op jit(solution)/shard_map/convert_element_type | solution.py:55
  (14 shorter events, 0.2 us)
Async XLA Ops:
  8.0 1.1 copy-start
  8.0 7.6 %copy-start.2 = (bf16[1,1,16,2,128,128]{5,4,3,2,1,0:T(8,128)(2,1)S(1)}, bf16[1,1,16,2,128,128]{5,4,3,2,1,0:T(8,128)(2,1)}, u32[]{:S(2)}) copy-start(bf16[1,1,16,2,128,128]{5,4,3,2,1,0:T(8,128)(2,1)} %param.13) | copy-start | bytes 3145732
  8.0 67.7 %all-gather.2.cloned.1.call-start = ((), (), s32[]{:S(2)}) async-start(), calls=%async_computation.1 | async-start | bytes 2228224 | tf_op jit(solution)/shard_map/all_gather | solution.py:45
  9.2 69.8 %copy-start.1 = (bf16[256,256]{1,0:T(8,128)(2,1)}, bf16[256,256]{1,0:T(8,128)(2,1)S(1)}, u32[]{:S(2)}) copy-start(bf16[256,256]{1,0:T(8,128)(2,1)S(1)} %compare_select_fusion) | copy-start | bytes 393220
  10.1 140.0 %all-reduce.2.cloned.1.call-start = ((), (), s32[]{:S(2)}) async-start(), calls=%async_computation.3 | async-start | bytes 524288 | tf_op jit(solution)/shard_map/psum | solution.py:56
  12.0 139.9 %reduce-scatter.2.cloned.1.call-start = ((), (), s32[]{:S(2)}) async-start(), calls=%async_computation.2 | async-start | bytes 786432 | tf_op jit(solution)/shard_map/reduce_scatter | solution.py:53
Sparse Core Ops, SparseCore 0:
  12.2 63.4 all-gather.1
  99.3 6.6 reduce-scatter.1
Sparse Core Ops, SparseCore 1:
  17.5 132.5 all-reduce.1
where the time goes:
time: 161 us
  waiting for transfers between devices  111 us (69%)
  between operations  15.6 us (10%)
  local copies, waits for them, and re-layouts  13.7 us (9%)
  other arithmetic  12.8 us (8%)
  matrix products  7.62 us (5%)
    all_gather x1, waiting for transfers between devices, body(): lax.all_gather(back_agg, 'graph', axis=0, tiled=True)  60 us
    psum x1, waiting for transfers between devices, body(): weight_grad = lax.psum(partial_weight, ('graph', 'rep'))  51 us
    scatter-add x2, other arithmetic, tile_products(): running.at[local_col[:, slot_index]].add(product * alive[:, None, None])  5.67 us
    gather x2, local copies, waits for them, and re-layouts, tile_products(): chosen = blocks[part_index, local_row[:, slot_index]]  5.41 us
    dot_general x2, matrix products, tile_products(): jnp.einsum('kab,kac->kbc', local_tiles[:, slot_index], chosen, preferred_...  4.91 us
    mul x2, local copies, waits for them, and re-layouts, tile_products(): product * alive[:, None, None]  4.82 us
  transfers between devices with their start and end apart: 3, of which 2 were waited for; matrix products, arithmetic and copies ran while one was open for 19% of the time, Pallas kernels for 0%

commit v1 on v0

--- a/solution.py
+++ b/solution.py
@@ -53,7 +53,7 @@
     input_grad = lax.psum_scatter(
         jnp.take(partial_grad, local_perm, axis=0), "rep", scatter_dimension=0, tiled=True
     ).astype(jnp.bfloat16)
-    weight_grad = lax.psum(partial_weight, ("graph", "rep"))
+    weight_grad = lax.psum(lax.psum(partial_weight, "rep"), "graph")
     return (input_grad, weight_grad, relu_grad)
 
 

time: 161 us -> 199 us (1.24)
  waiting for transfers between devices: 111 us -> 156 us
  other arithmetic: 12.8 us -> 9.33 us
  matrix products: 7.62 us -> 5.07 us
    psum x1 -> x2, waiting for transfers between devices: 51 us -> 111 us  [body(): weight_grad = lax.psum(lax.psum(partial_weight, 'rep'), 'graph')]
    all_gather x1, waiting for transfers between devices: 60 us -> 44.9 us  [body(): lax.all_gather(back_agg, 'graph', axis=0, tiled=True)]
    dot_general x2, matrix products: 4.91 us -> 2.36 us  [tile_products(): jnp.einsum('kab,kac->kbc', local_tiles[:, slot_index], chosen, preferred_...]
  transfers between devices with their start and end apart: 3 -> 4, of which waited for: 2 -> 3; matrix products, arithmetic and copies ran while one was open for 19% -> 12% of each run, Pallas kernels for 0% -> 0%
where the time goes in v1:
time: 199 us
  waiting for transfers between devices  156 us (78%)
  between operations  15.7 us (8%)
  local copies, waits for them, and re-layouts  12.7 us (6%)
  other arithmetic  9.33 us (5%)
  matrix products  5.07 us (3%)
    psum x2, waiting for transfers between devices, body(): weight_grad = lax.psum(lax.psum(partial_weight, 'rep'), 'graph')  111 us
    all_gather x1, waiting for transfers between devices, body(): lax.all_gather(back_agg, 'graph', axis=0, tiled=True)  44.9 us
    scatter-add x2, other arithmetic, tile_products(): running.at[local_col[:, slot_index]].add(product * alive[:, None, None])  5.66 us
    gather x2, local copies, waits for them, and re-layouts, tile_products(): chosen = blocks[part_index, local_row[:, slot_index]]  5.39 us
  transfers between devices with their start and end apart: 4, of which 3 were waited for; matrix products, arithmetic and copies ran while one was open for 12% of the time, Pallas kernels for 0%

profile of v1, /device:TPU:0, one launch (start us, length us, event | category | flops | bytes accessed | tf_op | source)
XLA Modules:
  0.0 198.7 jit_solution(11421232762565708792)
XLA Ops:
  8.1 0.0 all-reduce.3.cloned.1.call-start
  8.1 1.1 compare_select_fusion
  9.2 0.9 convolution_bitcast_fusion
  10.2 0.0 all-gather.2.cloned.1.call-start
  10.2 1.8 convolution_convert_fusion
  12.0 0.0 all-gather.2.cloned.1.call-update
  12.0 0.0 all-reduce.5.cloned.1.call-start
  12.1 0.1 copy.25
  12.3 20.5 %all-reduce.3.cloned.1.call-done = f32[256,256]{0,1:T(8,128)} async-done(((f32[256,256]{0,1:T(8,128)}), f32[256,256]{0,1:T(8,128)}) %all-reduce.3.cloned.1.call-update) | async-done | bytes 262160 | tf_op jit(solution)/shard_map/psum | solution.py:56
  32.8 0.0 reduce-scatter.2.cloned.1.call-start
  32.9 44.9 %all-gather.2.cloned.1.call-done = bf16[4096,256]{1,0:T(8,128)(2,1)} async-done(((bf16[256,256]{1,0:T(8,128)(2,1)}), bf16[4096,256]{1,0:T(8,128)(2,1)}) %all-gather.2.cloned.1.call-update) | async-done | bytes 2097168 | tf_op jit(solution)/shard_map/all_gather | solution.py:45
  77.8 2.2 %gather_fusion.1 = bf16[16,128,256]{2,1,0:T(8,128)(2,1)S(1)} fusion(bf16[16,2,128,256]{3,2,1,0:T(8,128)(2,1)} %bitcast.44, s32[16]{0:T(128)S(1)} %get-tuple-element.9), kind=kCustom, calls=%fused_computation.1 | custom fusion | bytes 2097280 | tf_op jit(solution)/shard_map/gather | solution.py:14
  80.0 3.2 %gather_fusion = bf16[16,128,256]{2,1,0:T(8,128)(2,1)} fusion(bf16[16,2,128,256]{3,2,1,0:T(8,128)(2,1)} %bitcast.45, s32[16]{0:T(128)S(1)} %get-tuple-element.10), kind=kCustom, calls=%fused_computation | custom fusion | bytes 2097280 | tf_op jit(solution)/shard_map/gather | solution.py:14
  83.2 1.8 multiply_bitcast_fusion
  85.0 0.5 multiply_bitcast_fusion.1
  85.6 1.8 copy.18
  87.4 1.9 copy.20
  89.4 3.5 %scatter_fusion = f32[4,128,256]{2,1,0:T(8,128)S(1)} fusion(f32[4,128,256]{2,1,0:T(8,128)S(1)} %broadcast_in_dim.10, s32[16]{0:T(128)S(1)} %get-tuple-element.12, f32[16,128,256]{2,1,0:T(8,128)} %copy.18), kind=kCustom, calls=%fused_computation.3 | custom fusion | flops 524288 | bytes 6291520 | tf_op jit(solution)/shard_map/scatter-add | solution.py:19
  92.8 2.2 %scatter_fusion.1 = f32[4,128,256]{2,1,0:T(8,128)S(1)} fusion(f32[4,128,256]{2,1,0:T(8,128)S(1)} %scatter_fusion, s32[16]{0:T(128)S(1)} %get-tuple-element.11, f32[16,128,256]{2,1,0:T(8,128)S(1)} %copy.20), kind=kCustom, calls=%fused_computation.4 | custom fusion | flops 524288 | bytes 6291520 | tf_op jit(solution)/shard_map/scatter-add | solution.py:19
  95.0 1.6 gather_fusion.2
  96.6 0.9 broadcast_select_fusion
  97.6 90.3 %all-reduce.5.cloned.1.call-done = f32[256,256]{0,1:T(8,128)} async-done(((f32[256,256]{0,1:T(8,128)}), f32[256,256]{0,1:T(8,128)}) %all-reduce.5.cloned.1.call-update) | async-done | bytes 262160 | tf_op jit(solution)/shard_map/psum | solution.py:56
  187.9 1.8 copy.21
  189.7 1.6 convert_element_type.31
  (27 shorter events, 0.2 us)
Async XLA Ops:
  8.0 1.2 copy-start
  8.0 4.1 %copy-start.3 = (bf16[1,1,16,2,128,128]{5,4,3,2,1,0:T(8,128)(2,1)S(1)}, bf16[1,1,16,2,128,128]{5,4,3,2,1,0:T(8,128)(2,1)}, u32[]{:S(2)}) copy-start(bf16[1,1,16,2,128,128]{5,4,3,2,1,0:T(8,128)(2,1)} %param.13) | copy-start | bytes 3145732
  8.0 4.2 %copy-start.4 = (s32[1,512]{1,0:T(1,128)S(1)}, s32[1,512]{1,0:T(1,128)}, u32[]{:S(2)}) copy-start(s32[1,512]{1,0:T(1,128)} %param.17) | copy-start | bytes 6148
  8.0 4.2 %copy-start.7 = (s32[1,1,16]{2,1,0:T(1,128)S(1)}, s32[1,1,16]{2,1,0:T(1,128)}, u32[]{:S(2)}) copy-start(s32[1,1,16]{2,1,0:T(1,128)} %param.16) | copy-start | bytes 196
  8.0 4.2 %copy-start.5 = (s32[1,1,16,2]{2,3,1,0:T(2,128)S(1)}, s32[1,1,16,2]{2,3,1,0:T(2,128)}, u32[]{:S(2)}) copy-start(s32[1,1,16,2]{2,3,1,0:T(2,128)} %param.14) | copy-start | bytes 388
  8.1 4.2 %copy-start.6 = (s32[1,1,16,2]{2,3,1,0:T(2,128)S(1)}, s32[1,1,16,2]{2,3,1,0:T(2,128)}, u32[]{:S(2)}) copy-start(s32[1,1,16,2]{2,3,1,0:T(2,128)} %param.15) | copy-start | bytes 388
  8.1 24.7 %all-reduce.3.cloned.1.call-start = ((), (), s32[]{:S(2)}) async-start(), calls=%async_computation.3 | async-start | bytes 524288 | tf_op jit(solution)/shard_map/psum | solution.py:56
  9.2 70.8 %copy-start.2 = (bf16[256,256]{1,0:T(8,128)(2,1)}, bf16[256,256]{1,0:T(8,128)(2,1)S(1)}, u32[]{:S(2)}) copy-start(bf16[256,256]{1,0:T(8,128)(2,1)S(1)} %compare_select_fusion) | copy-start | bytes 393220
  10.2 67.6 %all-gather.2.cloned.1.call-start = ((), (), s32[]{:S(2)}) async-start(), calls=%async_computation.1 | async-start | bytes 2228224 | tf_op jit(solution)/shard_map/all_gather | solution.py:45
  12.0 175.9 %all-reduce.5.cloned.1.call-start = ((), (), s32[]{:S(2)}) async-start(), calls=%async_computation.4 | async-start | bytes 524288 | tf_op jit(solution)/shard_map/psum | solution.py:56
  32.8 156.8 %reduce-scatter.2.cloned.1.call-start = ((), (), s32[]{:S(2)}) async-start(), calls=%async_computation.2 | async-start | bytes 786432 | tf_op jit(solution)/shard_map/reduce_scatter | solution.py:53
  83.2 1.9 copy-start.1
Sparse Core Ops, SparseCore 0:
  11.8 20.9 all-reduce.2
  97.7 6.7 reduce-scatter.1
Sparse Core Ops, SparseCore 1:
  14.4 63.3 all-gather.1
  82.9 105.0 all-reduce.4
